TPU v7x, 32 devices: a whole 2x2x4 slice. The times are simulated.
32 devices in a mesh: groups: 2 (over y), blk: 4 (over z), chan: 4 (over x, core).
Axes of the slice: x: 2, y: 2, z: 4, core: 2. Of those that a mesh axis runs over, the one named last changes fastest.
Arguments:
- fmap1: bfloat16 [128, 256, 128], P(('groups', 'blk'), 'chan'), parts along dimension 0, may hold values from -6 to 6
- fmap2: bfloat16 [128, 256, 128], P(('groups', 'blk'), 'chan'), parts along dimension 0, may hold values from -6 to 6
- windows: int32 [128, 20], P(('groups', 'blk')), parts along dimension 0, may hold values from 0 to 63, as said below
- live: int32 [128], P(('groups', 'blk')), parts along dimension 0, may hold values from 1 to 20, as said below
- cotangent: bfloat16 [128, 20, 128, 128], P(('groups', 'blk')), parts along dimension 0, may hold values from -6 to 6
Outputs:
- grad_one: float32 [128, 256, 128], P(('groups', 'blk'), 'chan'), parts along dimension 0
- grad_two: float32 [128, 256, 128], P(('groups', 'blk'), 'chan'), parts along dimension 0
There are 2 independent parts, one for each index of `groups`. A program takes and returns all parts, laid end to end along the dimension named above; each array names one. Nothing has to cross between parts.
Inputs may be any that keep to these rules, and one draw needn't show every extreme that they name: `windows`: the ids in one row are distinct; they may name blocks anywhere in the frame. Entries at slots live[b] and beyond are padding and carry no weight. `live`: some block uses all 20 slots.
All inputs are finite; a program needn't handle non-finite values.
Results may differ from a plain program's by a relative error of at most 0.0003.
Values may be sent and summed in bfloat16 or wider, within the bound.
A program may use at most 64 MiB of HBM per device.

v0:
```python
import math
import jax
import jax.numpy as jnp
from jax import lax
from jax.sharding import PartitionSpec as P

C = 256


def body(fmap1, fmap2, windows, live, cotangent):
    blocks, channels, site_count = fmap1.shape
    slot_count = windows.shape[1]
    inv_root = 1.0 / math.sqrt(C)
    slot_mask = (jnp.arange(slot_count, dtype=jnp.int32)[None, :] < live[:, None]).astype(
        jnp.float32
    )
    terms = jnp.einsum("bwij,bci->bwcj", cotangent, fmap1, preferred_element_type=jnp.float32)
    terms = terms * (inv_root * slot_mask)[:, :, None, None]
    flat_terms = terms.reshape(blocks * slot_count, channels * site_count)
    flat_ids = windows.reshape(-1)
    piece = lax.all_gather(fmap2, "blk", axis=0, tiled=True)
    piece_rows = piece.shape[0]
    row_ids = jnp.arange(piece_rows, dtype=jnp.int32)
    picker = (flat_ids[:, None] == row_ids[None, :]).astype(jnp.bfloat16)
    fetched = jnp.dot(
        picker, piece.reshape(piece_rows, channels * site_count), preferred_element_type=jnp.float32
    )
    fetched = fetched.astype(jnp.bfloat16).reshape(blocks, slot_count, channels, site_count)
    row_count = blocks * lax.axis_size("blk")
    row_ids = jnp.arange(row_count, dtype=jnp.int32)
    owner_hot = (row_ids[:, None] == flat_ids[None, :]).astype(jnp.float32)
    summed = jnp.dot(
        owner_hot, flat_terms, preferred_element_type=jnp.float32, precision=lax.Precision.HIGHEST
    )
    grad_two = lax.psum_scatter(
        summed.reshape(row_count, channels, site_count), "blk", scatter_dimension=0, tiled=True
    )
    selected = fetched * slot_mask.astype(jnp.bfloat16)[:, :, None, None]
    grad_one = (
        jnp.einsum("bwij,bwcj->bci", cotangent, selected, preferred_element_type=jnp.float32)
        * inv_root
    )
    return (grad_one, grad_two)


def solution(mesh):
    placed = (
        P(("groups", "blk"), "chan", None),
        P(("groups", "blk"), "chan", None),
        P(("groups", "blk"), None),
        P(("groups", "blk")),
        P(("groups", "blk"), None, None, None),
    )
    return jax.shard_map(
        body,
        mesh=mesh,
        in_specs=placed,
        out_specs=(P(("groups", "blk"), "chan", None), P(("groups", "blk"), "chan", None)),
        check_vma=False,
    )
```

profile of v0, /device:TPU:0, one launch (start us, length us, event | category | flops | bytes accessed | tf_op | source)
XLA Modules:
  0.0 94.8 jit_solution(12129404039623603795)
XLA Ops:
  7.2 0.0 copy-start
  7.2 0.0 all-gather.2.cloned.1.call-start
  7.2 0.7 all-gather.2.cloned.1.call-update
  7.9 0.0 reduce-scatter.2.cloned.1.call-start
  8.0 0.8 eq.28
  8.7 0.7 fusion.20
  9.5 0.0 copy-done
  9.5 4.9 %broadcast_multiply_fusion = f32[16,64,20,128]{3,1,2,0:T(8,128)S(1)} fusion(f32[16,20]{1,0:T(8,128)S(1)} %fusion.20, bf16[16,20,128,128]{3,2,1,0:T(8,128)(2,1)} %param.9, bf16[16,64,128]{2,1,0:T(8,128)(2,1)S(1)} %copy-done), kind=kOutput, calls=%fused_computation.5 | convolution fusion | flops 673710080 | bytes 21234944 | tf_op jit(solution)/shard_map/bwij,bci->bwcj/dot_general | solution.py:17
  14.4 0.0 copy-start.1
  14.4 11.9 %fusion = f32[64,64,128]{2,0,1:T(8,128)} fusion(s32[320]{0:T(512)S(1)} %eq.28, f32[40,8,64,128]{3,2,1,0:T(8,128)S(1)} %bitcast.38), kind=kOutput, calls=%fused_computation.2 | convolution fusion | flops 2013286400 | bytes 12584192 | tf_op jit(solution)/shard_map/dot_general | solution.py:32
  26.3 0.0 reduce-scatter.2.cloned.1.call-update
  26.3 0.0 copy-done.1
  26.3 0.1 convert_convert_fusion
  26.4 13.9 %all-gather.2.cloned.1.call-done = bf16[64,64,128]{2,1,0:T(8,128)(2,1)} async-done(((bf16[16,64,128]{2,1,0:T(8,128)(2,1)}), bf16[64,64,128]{2,1,0:T(8,128)(2,1)}) %all-gather.2.cloned.1.call-update) | async-done | bytes 1048592 | tf_op jit(solution)/shard_map/all_gather | solution.py:21
  40.2 2.8 %fusion.6 = bf16[40,8,64,128]{3,1,2,0:T(8,128)(2,1)S(1)} fusion(bf16[8,8,64,128]{3,2,1,0:T(8,128)(2,1)} %bitcast.40, s32[320]{0:T(512)S(1)} %eq.28), kind=kOutput, calls=%fused_computation.9 | convolution fusion | flops 338186240 | bytes 6292736 | tf_op jit(solution)/shard_map/dot_general | solution.py:25
  43.0 1.7 %copy.16 = bf16[40,8,64,128]{3,2,1,0:T(8,128)(2,1)S(1)} copy(bf16[40,8,64,128]{3,1,2,0:T(8,128)(2,1)S(1)} %fusion.6) | data formatting | bytes 10485760
  44.7 8.9 %fusion.10 = f32[16,64,128]{2,1,0:T(8,128)} fusion(bf16[16,20,128,128]{3,2,1,0:T(8,128)(2,1)} %param.9, bf16[16,20,64,128]{3,2,1,0:T(8,128)(2,1)S(1)} %bitcast.39, bf16[16,20]{1,0:T(8,128)(2,1)S(1)} %convert_convert_fusion), kind=kOutput, calls=%fused_computation.11 | convolution fusion | flops 673841152 | bytes 16253568 | tf_op jit(solution)/shard_map/bwij,bwcj->bci/dot_general | solution.py:40
  53.6 32.3 %reduce-scatter.2.cloned.1.call-done = f32[16,64,128]{2,0,1:T(8,128)} async-done(((f32[64,64,128]{2,0,1:T(8,128)}), f32[16,64,128]{2,0,1:T(8,128)}) %reduce-scatter.2.cloned.1.call-update) | async-done | bytes 524304 | tf_op jit(solution)/shard_map/reduce_scatter | solution.py:35
  85.9 2.0 %copy.11 = f32[16,64,128]{2,1,0:T(8,128)} copy(f32[16,64,128]{2,0,1:T(8,128)} %reduce-scatter.2.cloned.1.call-done) | data formatting | bytes 1048576
Async XLA Ops:
  7.2 2.3 %copy-start = (bf16[16,64,128]{2,1,0:T(8,128)(2,1)S(1)}, bf16[16,64,128]{2,1,0:T(8,128)(2,1)}, u32[]{:S(2)}) copy-start(bf16[16,64,128]{2,1,0:T(8,128)(2,1)} %param.5) | copy-start | bytes 786436
  7.2 33.1 %all-gather.2.cloned.1.call-start = ((), (), s32[]{:S(2)}) async-start(), calls=%async_computation.1 | async-start | bytes 1310720 | tf_op jit(solution)/shard_map/all_gather | solution.py:21
  7.9 78.0 %reduce-scatter.2.cloned.1.call-start = ((), (), s32[]{:S(2)}) async-start(), calls=%async_computation.2 | async-start | bytes 2621440 | tf_op jit(solution)/shard_map/reduce_scatter | solution.py:35
  14.4 11.9 %copy-start.1 = (s32[16]{0:T(128)S(1)}, s32[16]{0:T(128)}, u32[]{:S(2)}) copy-start(s32[16]{0:T(128)} %param.8) | copy-start | bytes 196
Sparse Core Ops, SparseCore 0:
  9.6 30.6 all-gather.1
  42.5 43.3 reduce-scatter.1
where the time goes:
time: 95 us; the launch traced here: 94.8 us
  waiting for transfers between devices  46.9 us (49%)
  matrix products  28.5 us (30%)
  between operations  14.1 us (15%)
  local copies, waits for them, and re-layouts  4.45 us (5%)
    reduce_scatter x1, waiting for transfers between devices, body(): lax.psum_scatter(summed.reshape(row_count, channels, site_count), 'blk',...  32.3 us
    all_gather x1, waiting for transfers between devices, body(): piece = lax.all_gather(fmap2, 'blk', axis=0, tiled=True)  13.9 us
    dot_general x1, matrix products, body(): jnp.dot(owner_hot, flat_terms, preferred_element_type=jnp.float32, precis...  11.9 us
    dot_general x1, matrix products, body(): jnp.einsum('bwij,bwcj->bci', cotangent, selected, preferred_element_type=...  8.92 us
    dot_general x1, matrix products, body(): jnp.einsum('bwij,bci->bwcj', cotangent, fmap1, preferred_element_type=jnp...  4.93 us
    unnamed x6, local copies, waits for them, and re-layouts  3.67 us
    dot_general x1, matrix products, body(): jnp.dot(picker, piece.reshape(piece_rows, channels * site_count), preferr...  2.79 us
  transfers between devices with their start and end apart: 2, of which 2 were waited for; matrix products, arithmetic and copies ran while one was open for 33% of the time, Pallas kernels for 0%

commit v1 on v0

--- a/solution.py
+++ b/solution.py
@@ -5,6 +5,25 @@
 from jax.sharding import PartitionSpec as P
 
 C = 256
+
+
+def joined_along(blocks, dim):
+    blocks = jnp.moveaxis(blocks, 0, dim)
+    lengths = blocks.shape
+    return blocks.reshape(*lengths[:dim], lengths[dim] * lengths[dim + 1], *lengths[dim + 2 :])
+
+
+def doubled(shard, axis):
+    count, index = (lax.axis_size(axis), lax.axis_index(axis))
+    blocks, apart = (shard[None], 1)
+    while apart < count:
+        partner_block = lax.ppermute(blocks, axis, [(i, i ^ apart) for i in range(count)])
+        low = index & apart == 0
+        blocks = jnp.concatenate(
+            [jnp.where(low, blocks, partner_block), jnp.where(low, partner_block, blocks)]
+        )
+        apart *= 2
+    return blocks
 
 
 def body(fmap1, fmap2, windows, live, cotangent):
@@ -18,7 +37,7 @@
     terms = terms * (inv_root * slot_mask)[:, :, None, None]
     flat_terms = terms.reshape(blocks * slot_count, channels * site_count)
     flat_ids = windows.reshape(-1)
-    piece = lax.all_gather(fmap2, "blk", axis=0, tiled=True)
+    piece = joined_along(doubled(fmap2, "blk"), 0)
     piece_rows = piece.shape[0]
     row_ids = jnp.arange(piece_rows, dtype=jnp.int32)
     picker = (flat_ids[:, None] == row_ids[None, :]).astype(jnp.bfloat16)

time: 95 us -> 110 us (1.16)
  waiting for transfers between devices: 46.9 us -> 57 us
  starting transfers between devices: 0.08 us -> 5.93 us
  matrix products: 28.5 us -> 27.1 us
    ppermute x0 -> x2, waiting for transfers between devices: none -> 56.9 us  [doubled(): lax.ppermute(blocks, axis, [(i, i ^ apart) for i in range(count)])]
    reduce_scatter x1, waiting for transfers between devices: 32.3 us -> 0.01 us  [body(): lax.psum_scatter(summed.reshape(row_count, channels, site_count), 'blk',...]
    all_gather x1 -> x0, waiting for transfers between devices: 13.9 us -> none  [body(): piece = lax.all_gather(fmap2, 'blk', axis=0, tiled=True)]
    ppermute x0 -> x2, starting transfers between devices: none -> 5.89 us  [doubled(): lax.ppermute(blocks, axis, [(i, i ^ apart) for i in range(count)])]
    unnamed x6 -> x8, local copies, waits for them, and re-layouts: 3.67 us -> 3.51 us
  transfers between devices with their start and end apart: 2 -> 3, of which waited for: 2 -> 2; matrix products, arithmetic and copies ran while one was open for 33% -> 11% of each run, Pallas kernels for 0% -> 0%
where the time goes in v1:
time: 110 us
  waiting for transfers between devices  57 us (52%)
  matrix products  27.1 us (25%)
  between operations  14.1 us (13%)
  starting transfers between devices  5.93 us (5%)
  local copies, waits for them, and re-layouts  4.33 us (4%)
    ppermute x2, waiting for transfers between devices, doubled(): lax.ppermute(blocks, axis, [(i, i ^ apart) for i in range(count)])  56.9 us
    dot_general x1, matrix products, body(): jnp.dot(owner_hot, flat_terms, preferred_element_type=jnp.float32, precis...  11.9 us
    dot_general x1, matrix products, body(): jnp.einsum('bwij,bwcj->bci', cotangent, selected, preferred_element_type=...  8.56 us
    ppermute x2, starting transfers between devices, doubled(): lax.ppermute(blocks, axis, [(i, i ^ apart) for i in range(count)])  5.89 us
    dot_general x1, matrix products, body(): jnp.einsum('bwij,bci->bwcj', cotangent, fmap1, preferred_element_type=jnp...  4.94 us
    unnamed x8, local copies, waits for them, and re-layouts  3.51 us
  transfers between devices with their start and end apart: 3, of which 2 were waited for; matrix products, arithmetic and copies ran while one was open for 11% of the time, Pallas kernels for 0%

profile of v1, /device:TPU:0, one launch (start us, length us, event | category | flops | bytes accessed | tf_op | source)
XLA Modules:
  0.0 109.5 jit_solution(662155666734341930)
XLA Ops:
  7.2 0.0 copy-start
  7.2 0.0 reduce-scatter.2.cloned.1.call-start
  7.2 0.8 eq.34
  8.0 0.7 fusion.20
  8.8 0.0 copy-done
  8.8 4.9 %broadcast_multiply_fusion = f32[16,64,20,128]{3,1,2,0:T(8,128)S(1)} fusion(f32[16,20]{1,0:T(8,128)S(1)} %fusion.20, bf16[16,20,128,128]{3,2,1,0:T(8,128)(2,1)} %param.9, bf16[16,64,128]{2,1,0:T(8,128)(2,1)S(1)} %copy-done), kind=kOutput, calls=%fused_computation.5 | convolution fusion | flops 673710080 | bytes 21234944 | tf_op jit(solution)/shard_map/bwij,bci->bwcj/dot_general | solution.py:36
  13.7 0.0 copy-start.1
  13.7 0.0 copy-start.2
  13.7 11.9 %fusion = f32[64,64,128]{2,0,1:T(8,128)} fusion(s32[320]{0:T(512)S(1)} %eq.34, f32[40,8,64,128]{3,2,1,0:T(8,128)S(1)} %bitcast.42), kind=kOutput, calls=%fused_computation.2 | convolution fusion | flops 2013286400 | bytes 12584192 | tf_op jit(solution)/shard_map/dot_general | solution.py:51
  25.6 0.0 reduce-scatter.2.cloned.1.call-update
  25.6 0.0 copy-done.1
  25.6 3.1 %collective-permute-start = (bf16[1,16,64,128]{3,2,1,0:T(8,128)(2,1)S(1)}, bf16[1,16,64,128]{3,2,1,0:T(8,128)(2,1)S(1)}, u32[]{:S(2)}, u32[]{:S(2)}) collective-permute-start(bf16[1,16,64,128]{3,2,1,0:T(8,128)(2,1)S(1)} %bitcast.45), channel_id=1, source_target_pairs={{0,4},{4,0},{8,12},{12,8},{1,5},{5,1},{9,13},{13,9},{2,6},{6,2},{1... | collective-permute-start | bytes 786440 | tf_op jit(solution)/shard_map/ppermute | solution.py:20
  28.7 6.3 %collective-permute-done = bf16[1,16,64,128]{3,2,1,0:T(8,128)(2,1)S(1)} collective-permute-done((bf16[1,16,64,128]{3,2,1,0:T(8,128)(2,1)S(1)}, bf16[1,16,64,128]{3,2,1,0:T(8,128)(2,1)S(1)}, u32[]{:S(2)}, u32[]{:S(2)}) %collective-permute-start) | collective-permute-done | bytes 262176 | tf_op jit(solution)/shard_map/ppermute | solution.py:20
  35.1 0.1 pad_maximum_fusion.1
  35.1 2.8 %collective-permute-start.1 = (bf16[2,16,64,128]{3,2,1,0:T(8,128)(2,1)S(1)}, bf16[2,16,64,128]{3,2,1,0:T(8,128)(2,1)S(1)}, u32[]{:S(2)}, u32[]{:S(2)}) collective-permute-start(bf16[2,16,64,128]{3,2,1,0:T(8,128)(2,1)S(1)} %pad_maximum_fusion.1), channel_id=1, source_target_pairs={{0,8},{4,12},{8,0},{12,4},{1,9},{5,13},{9,1},{13,5},{2,10},{6,14},... | collective-permute-start | bytes 1572872 | tf_op jit(solution)/shard_map/ppermute | solution.py:20
  38.0 0.0 copy-done.2
  38.0 0.1 convert_convert_fusion
  38.0 50.6 %collective-permute-done.1 = bf16[2,16,64,128]{3,2,1,0:T(8,128)(2,1)S(1)} collective-permute-done((bf16[2,16,64,128]{3,2,1,0:T(8,128)(2,1)S(1)}, bf16[2,16,64,128]{3,2,1,0:T(8,128)(2,1)S(1)}, u32[]{:S(2)}, u32[]{:S(2)}) %collective-permute-start.1) | collective-permute-done | bytes 524320 | tf_op jit(solution)/shard_map/ppermute | solution.py:20
  88.6 0.1 broadcast_select_fusion.1
  88.7 0.1 pad_maximum_fusion
  88.8 1.8 %fusion.6 = bf16[40,8,64,128]{3,1,2,0:T(8,128)(2,1)S(1)} fusion(bf16[8,8,64,128]{3,2,1,0:T(8,128)(2,1)S(1)} %bitcast.44, s32[320]{0:T(512)S(1)} %eq.34), kind=kOutput, calls=%fused_computation.9 | convolution fusion | flops 338186240 | bytes 6292736 | tf_op jit(solution)/shard_map/dot_general | solution.py:44
  90.6 1.5 %copy.14 = bf16[40,8,64,128]{3,2,1,0:T(8,128)(2,1)S(1)} copy(bf16[40,8,64,128]{3,1,2,0:T(8,128)(2,1)S(1)} %fusion.6) | data formatting | bytes 10485760
  92.1 8.6 %fusion.10 = f32[16,64,128]{2,1,0:T(8,128)} fusion(bf16[16,20,128,128]{3,2,1,0:T(8,128)(2,1)} %param.9, bf16[16,20,64,128]{3,2,1,0:T(8,128)(2,1)S(1)} %bitcast.43, bf16[16,20]{1,0:T(8,128)(2,1)S(1)} %convert_convert_fusion), kind=kOutput, calls=%fused_computation.11 | convolution fusion | flops 673841152 | bytes 16253568 | tf_op jit(solution)/shard_map/bwij,bwcj->bci/dot_general | solution.py:59
  100.7 0.0 reduce-scatter.2.cloned.1.call-done
  100.7 2.0 %copy.9 = f32[16,64,128]{2,1,0:T(8,128)} copy(f32[16,64,128]{2,0,1:T(8,128)} %reduce-scatter.2.cloned.1.call-done) | data formatting | bytes 1048576
  (1 shorter events, 0.0 us)
Async XLA Ops:
  7.2 1.6 %copy-start = (bf16[16,64,128]{2,1,0:T(8,128)(2,1)S(1)}, bf16[16,64,128]{2,1,0:T(8,128)(2,1)}, u32[]{:S(2)}) copy-start(bf16[16,64,128]{2,1,0:T(8,128)(2,1)} %param.5) | copy-start | bytes 786436
  7.2 93.5 %reduce-scatter.2.cloned.1.call-start = ((), (), s32[]{:S(2)}) async-start(), calls=%async_computation.1 | async-start | bytes 2621440 | tf_op jit(solution)/shard_map/reduce_scatter | solution.py:54
  13.7 11.9 %copy-start.1 = (bf16[16,64,128]{2,1,0:T(8,128)(2,1)S(1)}, bf16[16,64,128]{2,1,0:T(8,128)(2,1)}, u32[]{:S(2)}) copy-start(bf16[16,64,128]{2,1,0:T(8,128)(2,1)} %param.6) | copy-start | bytes 786436
  13.7 24.2 %copy-start.2 = (s32[16]{0:T(128)S(1)}, s32[16]{0:T(128)}, u32[]{:S(2)}) copy-start(s32[16]{0:T(128)} %param.8) | copy-start | bytes 196
  25.6 9.4 %collective-permute-start = (bf16[1,16,64,128]{3,2,1,0:T(8,128)(2,1)S(1)}, bf16[1,16,64,128]{3,2,1,0:T(8,128)(2,1)S(1)}, u32[]{:S(2)}, u32[]{:S(2)}) collective-permute-start(bf16[1,16,64,128]{3,2,1,0:T(8,128)(2,1)S(1)} %bitcast.45), channel_id=1, source_target_pairs={{0,4},{4,0},{8,12},{12,8},{1,5},{5,1},{9,13},{13,9},{2,6},{6,2},{1... | collective-permute-start | bytes 786440 | tf_op jit(solution)/shard_map/ppermute | solution.py:20
  35.1 53.5 %collective-permute-start.1 = (bf16[2,16,64,128]{3,2,1,0:T(8,128)(2,1)S(1)}, bf16[2,16,64,128]{3,2,1,0:T(8,128)(2,1)S(1)}, u32[]{:S(2)}, u32[]{:S(2)}) collective-permute-start(bf16[2,16,64,128]{3,2,1,0:T(8,128)(2,1)S(1)} %pad_maximum_fusion.1), channel_id=1, source_target_pairs={{0,8},{4,12},{8,0},{12,4},{1,9},{5,13},{9,1},{13,5},{2,10},{6,14},... | collective-permute-start | bytes 1572872 | tf_op jit(solution)/shard_map/ppermute | solution.py:20
Sparse Core Ops, SparseCore 0:
  25.7 66.2 reduce-scatter.1
